TPU v7x, 32 devices: a whole 2x2x4 slice. The times are simulated.
32 devices in a mesh: grp: 4 (over y, x), hh: 8 (over z, core).
Axes of the slice: x: 2, y: 2, z: 4, core: 2. Of those that a mesh axis runs over, the one named last changes fastest.
Arguments:
- hh_factors: bfloat16 [8192, 256], P('hh')
- prod_init: float32 [6144, 256], P(('grp', 'hh')), may hold values from -1.2 to 1.2
- hh_index: int32 [4, 192, 8, 8, 8], P('grp', None, None, 'hh'), may hold values from 0 to 1023
- trips: int32 [4, 192, 8, 8, 8], P('grp', None, None, 'hh'), may hold values from 1 to 8
- counts: int32 [4, 192, 8, 8], P('grp', None, None, 'hh'), may hold values from 0 to 8, as said below
Outputs:
- prod_factors: float32 [6144, 256], P(('grp', 'hh'))
Inputs may be any that keep to these rules, and one draw needn't show every extreme that they name: `hh_index`: a household row within its owner's shard. `counts`: live slots of one product from one source shard; 8 is reached in every draw.
All inputs are finite; a program needn't handle non-finite values.
Results may differ from a plain program's by a relative error of at most 0.0003.
The roundings to bfloat16 on the way count: a program that leaves them out, or rounds other values in their place, can miss the bound.
Values may be sent and summed in bfloat16 or wider, within the bound.
A program may use at most 128 MiB of HBM per device.

v0:
```python
import jax
import jax.numpy as jnp
from jax import lax
from jax.sharding import PartitionSpec as P

conf_scale = 40.0
ridge_term = 16.0
small_eps = 1e-06


def apply_system(gram, factors, weighted, vector):
    dense = jnp.dot(vector, gram, precision=lax.Precision.HIGHEST)
    inner = jnp.einsum(
        "plm,pm->pl", weighted.astype(jnp.float32), vector, precision=lax.Precision.HIGHEST
    )
    spread = jnp.einsum(
        "plk,pl->pk", factors.astype(jnp.float32), inner, precision=lax.Precision.HIGHEST
    )
    return dense + spread + ridge_term * vector


def shards(hh_factors, prod_init, hh_index, trips, counts):
    width = hh_factors.shape[1]
    shard_rows = hh_factors.shape[0]
    prod_count = prod_init.shape[0]
    sources = lax.axis_size("hh")
    slots_cap = hh_index.shape[4]
    group_rows = shard_rows // lax.axis_size("grp")
    row_start = lax.axis_index("grp") * group_rows
    gram_rows = lax.dynamic_slice_in_dim(hh_factors, row_start, group_rows, 0)
    gram_local = lax.dot_general(
        gram_rows, gram_rows, (((0,), (0,)), ((), ())), preferred_element_type=jnp.float32
    )
    gram = lax.psum(gram_local, ("grp", "hh"))
    picked = jnp.take(hh_factors, hh_index.reshape(-1), axis=0).reshape(hh_index.shape + (width,))
    got_rows, trips_in, counts_in = (
        lax.all_to_all(picked, "hh", split_axis=2, concat_axis=3, tiled=True),
        lax.all_to_all(trips, "hh", split_axis=2, concat_axis=3, tiled=True),
        lax.all_to_all(counts, "hh", split_axis=2, concat_axis=3, tiled=True),
    )
    slot_total = sources * slots_cap
    factors = got_rows.reshape(prod_count, slot_total, width)
    trips_flat = trips_in.reshape(prod_count, sources, slots_cap)
    counts_flat = counts_in.reshape(prod_count, sources, 1)
    slot_ids = lax.broadcasted_iota(jnp.int32, (prod_count, sources, slots_cap), 2)
    live = (slot_ids < counts_flat).astype(jnp.float32).reshape(prod_count, slot_total)
    weight = (
        conf_scale
        * jnp.log1p(trips_flat.astype(jnp.float32)).reshape(prod_count, slot_total)
        * live
    )
    weighted = (weight[:, :, None] * factors.astype(jnp.float32)).astype(jnp.bfloat16)
    coef = (live * (1.0 + weight)).astype(jnp.bfloat16)
    rhs = jnp.einsum("pl,plk->pk", coef, factors, preferred_element_type=jnp.float32)
    solution = prod_init
    resid = rhs - apply_system(gram, factors, weighted, solution)
    direc = resid
    norm_now = jnp.sum(resid * resid, axis=-1)
    for turn_idx in range(2):
        image = apply_system(gram, factors, weighted, direc)
        alpha = norm_now / (jnp.sum(direc * image, axis=-1) + small_eps)
        solution = solution + alpha[:, None] * direc
        resid = resid - alpha[:, None] * image
        norm_next = jnp.sum(resid * resid, axis=-1)
        direc = resid + (norm_next / (norm_now + small_eps))[:, None] * direc
        norm_now = norm_next
    return solution


def solution(mesh):
    placed = (
        P("hh", None),
        P(("grp", "hh"), None),
        P("grp", None, None, "hh", None),
        P("grp", None, None, "hh", None),
        P("grp", None, None, "hh"),
    )
    return jax.shard_map(
        shards, mesh=mesh, in_specs=placed, out_specs=P(("grp", "hh"), None), check_vma=False
    )
```

profile of v0, /device:TPU:0, one launch (start us, length us, event | category | flops | bytes accessed | tf_op | source)
XLA Modules:
  0.0 287.9 jit_solution(15379933742418415058)
XLA Ops:
  6.5 0.0 copy-start
  6.5 6.5 %all-to-all-start = ((s32[1,192,8,1]{1,3,0,2:T(1,128)}), s32[1,192,8,1]{1,3,0,2:T(1,128)S(1)}, u32[]{:S(2)}, u32[]{:S(2)}) async-start(s32[1,192,8,1]{1,3,0,2:T(1,128)} %bitcast.104), calls=%async_computation | async-start | bytes 16384 | tf_op jit(solution)/shard_map/all_to_all | solution.py:39
  13.0 1.2 copy.28
  14.2 0.4 reshape.130
  14.6 0.1 compare_select_fusion
  14.6 0.9 compare_and_fusion
  15.5 0.4 copy.27
  15.9 0.0 copy-done
  15.9 48.8 %gather_fusion = bf16[12288,256]{1,0:T(8,128)(2,1)} fusion(bf16[1024,256]{1,0:T(8,128)(2,1)S(1)} %copy-done, s32[12288]{0:T(1024)S(1)} %broadcast_clamp_fusion), kind=kCustom, calls=%fused_computation | custom fusion | bytes 12632064 | tf_op jit(solution)/shard_map/jit(_take)/gather | solution.py:35
  64.7 0.0 all-to-all-done
  64.7 5.1 %all-to-all-start.1 = ((s32[1,192,8,1,8]{1,4,3,0,2:T(8,128)}), s32[1,192,8,1,8]{1,4,3,0,2:T(8,128)S(1)}, u32[]{:S(2)}, u32[]{:S(2)}) async-start(s32[1,192,8,1,8]{1,4,3,0,2:T(8,128)} %bitcast.2), calls=%async_computation.1 | async-start | bytes 131072 | tf_op jit(solution)/shard_map/all_to_all | solution.py:38
  69.8 7.7 %copy_select_fusion = bf16[1,192,8,1,8,256]{5,4,1,3,0,2:T(8,128)(2,1)} fusion(bf16[1,192,8,1,8,256]{5,4,2,1,3,0:T(8,128)(2,1)} %bitcast.99, pred[192,8,8]{2,0,1:T(8,128)(4,1)S(1)} %copy.27), kind=kLoop, calls=%fused_computation.10 | loop fusion | flops 3145728 | bytes 12595200 | tf_op jit(solution)/shard_map/jit(_take)/select_n | solution.py:35
  77.5 0.0 copy-start.2
  77.5 0.0 all-to-all-done.1
  77.5 5.2 %all-to-all-start.2 = ((bf16[1,192,8,1,8,256]{5,4,1,3,0,2:T(8,128)(2,1)}), bf16[1,192,8,1,8,256]{5,4,1,3,0,2:T(8,128)(2,1)}, u32[]{:S(2)}, u32[]{:S(2)}) async-start(bf16[1,192,8,1,8,256]{5,4,1,3,0,2:T(8,128)(2,1)} %copy_select_fusion), calls=%async_computation.2 | async-start | bytes 12582912 | tf_op jit(solution)/shard_map/all_to_all | solution.py:37
  82.7 0.2 all-reduce.2.cloned.1.call-start
  83.0 0.9 fusion.31
  83.9 0.0 all-reduce.2.cloned.1.call-update
  83.9 0.1 iota.12
  84.0 0.1 fusion.35
  84.1 0.1 copy.31
  84.2 0.1 copy.32
  84.3 140.3 %all-to-all-done.2 = bf16[1,192,8,1,8,256]{5,4,1,3,0,2:T(8,128)(2,1)} async-done(((bf16[1,192,8,1,8,256]{5,4,1,3,0,2:T(8,128)(2,1)}), bf16[1,192,8,1,8,256]{5,4,1,3,0,2:T(8,128)(2,1)}, u32[]{:S(2)}, u32[]{:S(2)}) %all-to-all-start.2) | async-done | bytes 6291488 | tf_op jit(solution)/shard_map/all_to_all | solution.py:37
  224.6 0.0 copy-done.2
  224.6 7.1 %fusion.25 = f32[192,64,1]{1,2,0:T(1,128)S(1)} fusion(f32[192,64]{1,0:T(8,128)S(1)} %copy.31, bf16[1,192,8,1,8,256]{5,4,1,3,0,2:T(8,128)(2,1)} %all-to-all-done.2, f32[192,256,1]{1,0,2:T(8,128)S(1)} %bitcast.101), kind=kOutput, calls=%fused_computation.31 | convolution fusion | flops 47185920 | bytes 6586368 | tf_op jit(solution)/shard_map/plm,pm->pl/dot_general | solution.py:13
  231.8 4.6 %fusion.4 = f32[192,1,256]{2,1,0:T(1,128)S(1)} fusion(f32[192,64,1]{1,2,0:T(1,128)S(1)} %fusion.25, bf16[1,192,8,1,8,256]{5,4,1,3,0,2:T(8,128)(2,1)} %all-to-all-done.2), kind=kOutput, calls=%fused_computation.6 | convolution fusion | flops 37748736 | bytes 6537216 | tf_op jit(solution)/shard_map/plk,pl->pk/dot_general | solution.py:16
  236.4 3.7 %fusion.6 = f32[192,1,256]{2,1,0:T(1,128)S(1)} fusion(bf16[192,64,1]{1,2,0:T(2,128)(2,1)S(1)} %copy.32, bf16[1,192,8,1,8,256]{5,4,1,3,0,2:T(8,128)(2,1)} %all-to-all-done.2), kind=kOutput, calls=%fused_computation.8 | convolution fusion | flops 6291456 | bytes 6512640 | tf_op jit(solution)/shard_map/pl,plk->pk/dot_general | solution.py:54
  240.1 13.9 %all-reduce.2.cloned.1.call-done = f32[256,256]{1,0:T(8,128)} async-done(((f32[256,256]{1,0:T(8,128)}), f32[256,256]{1,0:T(8,128)}) %all-reduce.2.cloned.1.call-update) | async-done | bytes 262160 | tf_op jit(solution)/shard_map/psum | solution.py:34
  254.0 1.3 fusion.23
  255.3 7.1 %fusion.26 = f32[192,64,1]{1,2,0:T(1,128)S(1)} fusion(f32[192,64]{1,0:T(8,128)S(1)} %copy.31, bf16[1,192,8,1,8,256]{5,4,1,3,0,2:T(8,128)(2,1)} %all-to-all-done.2, f32[192,256,1]{1,0,2:T(8,128)S(1)} %bitcast.100), kind=kOutput, calls=%fused_computation.32 | convolution fusion | flops 47185920 | bytes 6586368 | tf_op jit(solution)/shard_map/plm,pm->pl/dot_general | solution.py:13
  262.4 0.0 copy-start.1
  262.4 4.7 %fusion.2 = f32[192,1,256]{2,1,0:T(1,128)S(1)} fusion(f32[192,64,1]{1,2,0:T(1,128)S(1)} %fusion.26, bf16[1,192,8,1,8,256]{5,4,1,3,0,2:T(8,128)(2,1)} %all-to-all-done.2), kind=kOutput, calls=%fused_computation.4 | convolution fusion | flops 37748736 | bytes 6537216 | tf_op jit(solution)/shard_map/plk,pl->pk/dot_general | solution.py:16
  267.1 0.0 copy-done.1
  267.1 0.5 multiply_reduce_fusion.1
  267.6 0.2 multiply_reduce_fusion
  267.8 0.1 fusion.37
  268.0 7.1 %fusion.27 = f32[192,64,1]{1,2,0:T(1,128)S(1)} fusion(f32[192,64]{1,0:T(8,128)S(1)} %copy.31, bf16[1,192,8,1,8,256]{5,4,1,3,0,2:T(8,128)(2,1)} %all-to-all-done.2, f32[192,256,1]{1,0,2:T(8,128)S(1)} %fusion.37), kind=kOutput, calls=%fused_computation.33 | convolution fusion | flops 47185920 | bytes 6586368 | tf_op jit(solution)/shard_map/plm,pm->pl/dot_general | solution.py:13
  275.1 4.6 %fusion = f32[192,1,256]{2,1,0:T(1,128)S(1)} fusion(f32[192,64,1]{1,2,0:T(1,128)S(1)} %fusion.27, bf16[1,192,8,1,8,256]{5,4,1,3,0,2:T(8,128)(2,1)} %all-to-all-done.2), kind=kOutput, calls=%fused_computation.2 | convolution fusion | flops 37748736 | bytes 6537216 | tf_op jit(solution)/shard_map/plk,pl->pk/dot_general | solution.py:16
  279.7 0.5 fusion.24
  280.2 0.8 multiply_add_fusion
  (6 shorter events, 0.0 us)
Async XLA Ops:
  6.5 9.3 %copy-start = (bf16[1024,256]{1,0:T(8,128)(2,1)S(1)}, bf16[1024,256]{1,0:T(8,128)(2,1)}, u32[]{:S(2)}) copy-start(bf16[1024,256]{1,0:T(8,128)(2,1)} %param.5) | copy-start | bytes 1572868
  6.5 58.2 %all-to-all-start = ((s32[1,192,8,1]{1,3,0,2:T(1,128)}), s32[1,192,8,1]{1,3,0,2:T(1,128)S(1)}, u32[]{:S(2)}, u32[]{:S(2)}) async-start(s32[1,192,8,1]{1,3,0,2:T(1,128)} %bitcast.104), calls=%async_computation | async-start | bytes 16384 | tf_op jit(solution)/shard_map/all_to_all | solution.py:39
  64.7 12.8 %all-to-all-start.1 = ((s32[1,192,8,1,8]{1,4,3,0,2:T(8,128)}), s32[1,192,8,1,8]{1,4,3,0,2:T(8,128)S(1)}, u32[]{:S(2)}, u32[]{:S(2)}) async-start(s32[1,192,8,1,8]{1,4,3,0,2:T(8,128)} %bitcast.2), calls=%async_computation.1 | async-start | bytes 131072 | tf_op jit(solution)/shard_map/all_to_all | solution.py:38
  77.5 147.1 %copy-start.2 = (f32[192,256]{1,0:T(8,128)S(1)}, f32[192,256]{1,0:T(8,128)}, u32[]{:S(2)}) copy-start(f32[192,256]{1,0:T(8,128)} %param.6) | copy-start | bytes 589828
  77.5 147.1 %all-to-all-start.2 = ((bf16[1,192,8,1,8,256]{5,4,1,3,0,2:T(8,128)(2,1)}), bf16[1,192,8,1,8,256]{5,4,1,3,0,2:T(8,128)(2,1)}, u32[]{:S(2)}, u32[]{:S(2)}) async-start(bf16[1,192,8,1,8,256]{5,4,1,3,0,2:T(8,128)(2,1)} %copy_select_fusion), calls=%async_computation.2 | async-start | bytes 12582912 | tf_op jit(solution)/shard_map/all_to_all | solution.py:37
  82.7 171.3 %all-reduce.2.cloned.1.call-start = ((), (), s32[]{:S(2)}) async-start(), calls=%async_computation.3 | async-start | bytes 524288 | tf_op jit(solution)/shard_map/psum | solution.py:34
  262.4 4.7 %copy-start.1 = (f32[256,256]{1,0:T(8,128)S(1)}, f32[256,256]{1,0:T(8,128)}, u32[]{:S(2)}) copy-start(f32[256,256]{1,0:T(8,128)} %all-reduce.2.cloned.1.call-done) | copy-start | bytes 786436
Sparse Core Ops, SparseCore 0:
  89.1 164.8 all-reduce.1
where the time goes:
time: 289 us; the launch traced here: 288 us
  waiting for transfers between devices  154 us (53%)
  local copies, waits for them, and re-layouts  51.1 us (18%)
  matrix products  42.2 us (15%)
  starting transfers between devices  17 us (6%)
  between operations  13.5 us (5%)
  other arithmetic  9.87 us (3%)
    all_to_all x1, waiting for transfers between devices, shards(): lax.all_to_all(picked, 'hh', split_axis=2, concat_axis=3, tiled=True)  140 us
    gather x1, local copies, waits for them, and re-layouts, shards(): jnp.take(hh_factors, hh_index.reshape(-1), axis=0)  48.8 us
    dot_general x3, matrix products, apply_system(): jnp.einsum('plm,pm->pl', weighted.astype(jnp.float32), vector, precision=...  21.4 us
    dot_general x3, matrix products, apply_system(): jnp.einsum('plk,pl->pk', factors.astype(jnp.float32), inner, precision=la...  13.9 us
    psum x1, waiting for transfers between devices, shards(): gram = lax.psum(gram_local, ('grp', 'hh'))  13.9 us
    select_n x2, other arithmetic, shards(): jnp.take(hh_factors, hh_index.reshape(-1), axis=0)  7.73 us
    all_to_all x1, starting transfers between devices, shards(): lax.all_to_all(counts, 'hh', split_axis=2, concat_axis=3, tiled=True)  6.46 us
  transfers between devices with their start and end apart: 4, of which 2 were waited for; matrix products, arithmetic and copies ran while one was open for 26% of the time, Pallas kernels for 0%

commit v1 on v0

v1 whole, which is shorter than its diff:
```python
import functools

import jax
import jax.numpy as jnp
from jax import lax
from jax.experimental import pallas as pl
from jax.experimental.pallas import tpu as pltpu
from jax.sharding import PartitionSpec as P

conf_scale = 40.0
ridge_term = 16.0
small_eps = 1e-06
half_word = 16

NN = (((1,), (0,)), ((), ()))
NT = (((1,), (1,)), ((), ()))


def dot(left, right, dims=NN):
    return lax.dot_general(left, right, dims, preferred_element_type=jnp.float32)


def halves(value):
    high = value.astype(jnp.bfloat16)
    low = (value - high.astype(jnp.float32)).astype(jnp.bfloat16)
    return high, low


def stacked(value):
    return jnp.concatenate(halves(value), axis=0)


def folded(value):
    rows = value.shape[0] // 2
    return value[:rows] + value[rows:]


def solve(code_ref, start_ref, table_ref, out_ref, gram_high, gram_low, rows_ref, weighted_ref, coef_ref):
    sources, width, households = table_ref.shape
    groups = rows_ref.shape[0]
    block = start_ref.shape[0]
    per_group = block // groups
    lanes = code_ref.shape[1] // groups
    cap = lanes // per_group

    @pl.when(pl.program_id(0) == 0)
    def _():
        gram = dot(table_ref[0], table_ref[0], NT)
        for source in range(1, sources):
            gram = gram + dot(table_ref[source], table_ref[source], NT)
        gram_high[...], gram_low[...] = halves(gram)

    household_ids = lax.broadcasted_iota(jnp.int32, (households, lanes), 0)

    def gather(source):
        table = table_ref[source]
        for group in range(groups):
            code = code_ref[pl.ds(source, 1), group * lanes : (group + 1) * lanes]
            trips = code >> half_word
            index = code & ((1 << half_word) - 1)
            weight = conf_scale * jnp.log1p(trips.astype(jnp.float32))
            live = (trips > 0).astype(jnp.float32)
            onehot = (household_ids == index).astype(jnp.float32).astype(jnp.bfloat16)
            picked = dot(table, onehot)
            place = pl.ds(pl.multiple_of(source * lanes, 128), lanes)
            rows_ref[group, :, place] = picked.astype(jnp.bfloat16)
            weighted_ref[group, :, place] = (weight * picked).astype(jnp.bfloat16)
            coef_ref[group, :, place] = (live * (1.0 + weight)).astype(jnp.bfloat16).astype(jnp.float32)

    pl.loop(0, sources)(gather)

    slots = sources * lanes
    row_ids = lax.broadcasted_iota(jnp.int32, (per_group, slots), 0)
    lane_ids = lax.broadcasted_iota(jnp.int32, (per_group, slots), 1)
    own = lax.rem(lane_ids, lanes) // cap == row_ids

    def spread(vector, from_coef):
        pieces = []
        for group in range(groups):
            part = vector[group * per_group : (group + 1) * per_group]
            inner = folded(dot(stacked(part), weighted_ref[group]))
            if from_coef:
                inner = coef_ref[group] - inner
            inner = jnp.where(own, inner, 0.0)
            pieces.append(folded(dot(stacked(inner), rows_ref[group], NT)))
        return jnp.concatenate(pieces, axis=0)

    def dense(vector):
        both = stacked(vector)
        return (
            folded(dot(both, gram_high[...]))
            + dot(both[: vector.shape[0]], gram_low[...])
            + ridge_term * vector
        )

    answer = start_ref[...]
    resid = spread(answer, True) - dense(answer)
    direc = resid
    norm_now = jnp.sum(resid * resid, axis=-1, keepdims=True)
    for turn in range(2):
        image = dense(direc) + spread(direc, False)
        alpha = norm_now / (jnp.sum(direc * image, axis=-1, keepdims=True) + small_eps)
        answer = answer + alpha * direc
        if turn == 0:
            resid = resid - alpha * image
            norm_next = jnp.sum(resid * resid, axis=-1, keepdims=True)
            direc = resid + (norm_next / (norm_now + small_eps)) * direc
            norm_now = norm_next
    out_ref[...] = answer


def shards(hh_factors, prod_init, hh_index, trips, counts):
    households, width = hh_factors.shape
    products = prod_init.shape[0]
    sources = lax.axis_size("hh")
    cap = hh_index.shape[4]
    table = lax.all_gather(hh_factors.T, "hh", axis=0)
    slot_ids = lax.broadcasted_iota(jnp.int32, hh_index.shape, 4)
    live_trips = jnp.where(slot_ids < counts[..., None], trips, 0)
    code = (live_trips << half_word) | hh_index
    code = code.reshape(products, sources, cap).transpose(1, 0, 2).reshape(sources, products * cap)
    code = lax.all_to_all(code, "hh", split_axis=0, concat_axis=0, tiled=True)

    per_group = 64 if products % 64 == 0 else products
    block = products if products * sources * cap <= 16384 else per_group
    groups = block // per_group
    lanes = per_group * cap
    return pl.pallas_call(
        solve,
        grid=(products // block,),
        out_shape=jax.ShapeDtypeStruct(prod_init.shape, jnp.float32),
        in_specs=[
            pl.BlockSpec((sources, block * cap), lambda i: (0, i)),
            pl.BlockSpec((block, width), lambda i: (i, 0)),
            pl.BlockSpec(memory_space=pltpu.VMEM),
        ],
        out_specs=pl.BlockSpec((block, width), lambda i: (i, 0)),
        scratch_shapes=[
            pltpu.VMEM((width, width), jnp.bfloat16),
            pltpu.VMEM((width, width), jnp.bfloat16),
            pltpu.VMEM((groups, width, sources * lanes), jnp.bfloat16),
            pltpu.VMEM((groups, width, sources * lanes), jnp.bfloat16),
            pltpu.VMEM((groups, 1, sources * lanes), jnp.float32),
        ],
        compiler_params=pltpu.CompilerParams(vmem_limit_bytes=60 * 2**20),
    )(code, prod_init, table)


def solution(mesh):
    placed = (
        P("hh", None),
        P(("grp", "hh"), None),
        P("grp", None, None, "hh", None),
        P("grp", None, None, "hh", None),
        P("grp", None, None, "hh"),
    )
    return jax.shard_map(
        shards, mesh=mesh, in_specs=placed, out_specs=P(("grp", "hh"), None), check_vma=False
    )
```

time: 289 us -> 98.6 us (0.34)
  waiting for transfers between devices: 154 us -> 38.1 us
  local copies, waits for them, and re-layouts: 51.1 us -> 8.43 us
  matrix products: 42.2 us -> 0 us
  Pallas kernels: 0 us -> 25.5 us
  starting transfers between devices: 17 us -> 0.01 us
  blocking collectives: 0 us -> 12 us
  other arithmetic: 9.87 us -> 0.89 us
    all_to_all x3 -> x0, waiting for transfers between devices: 140 us -> none  [the longest x1 140 us: shards(): lax.all_to_all(picked, 'hh', split_axis=2, concat_axis=3, tiled=True)]
    gather x1 -> x0, local copies, waits for them, and re-layouts: 48.8 us -> none  [shards(): jnp.take(hh_factors, hh_index.reshape(-1), axis=0)]
    dot_general x11 -> x0, matrix products: 42.2 us -> none  [the longest x3 21.4 us: apply_system(): jnp.einsum('plm,pm->pl', weighted.astype(jnp.float32), vector, precision=...]
    all_gather x0 -> x1, waiting for transfers between devices: none -> 37.4 us  [shards(): table = lax.all_gather(hh_factors.T, 'hh', axis=0)]
    pallas_call x0 -> x1, Pallas kernels: none -> 25.5 us  [shards(): pl.pallas_call(solve, grid=(products // block,), out_shape=jax.ShapeDtype...]
    all_to_all x3 -> x0, starting transfers between devices: 16.8 us -> none  [the longest x1 6.46 us: shards(): lax.all_to_all(counts, 'hh', split_axis=2, concat_axis=3, tiled=True)]
    psum x1 -> x0, waiting for transfers between devices: 13.9 us -> none  [shards(): gram = lax.psum(gram_local, ('grp', 'hh'))]
    all_to_all x0 -> x1, blocking collectives: none -> 12 us  [shards(): code = lax.all_to_all(code, 'hh', split_axis=0, concat_axis=0, tiled=True)]
  transfers between devices with their start and end apart: 4 -> 1, of which waited for: 2 -> 1; matrix products, arithmetic and copies ran while one was open for 26% -> 3% of each run, Pallas kernels for 0% -> 0%
where the time goes in v1:
time: 98.6 us; the launch traced here: 98.2 us
  waiting for transfers between devices  38.1 us (39%)
  Pallas kernels  25.5 us (26%)
  between operations  13.4 us (14%)
  blocking collectives  12 us (12%)
  local copies, waits for them, and re-layouts  8.43 us (9%)
    all_gather x1, waiting for transfers between devices, shards(): table = lax.all_gather(hh_factors.T, 'hh', axis=0)  37.4 us
    pallas_call x1, Pallas kernels, shards(): pl.pallas_call(solve, grid=(products // block,), out_shape=jax.ShapeDtype...  25.5 us
    all_to_all x1, blocking collectives, shards(): code = lax.all_to_all(code, 'hh', split_axis=0, concat_axis=0, tiled=True)  12 us
    all_gather x1, local copies, waits for them, and re-layouts, shards(): table = lax.all_gather(hh_factors.T, 'hh', axis=0)  6.42 us
  transfers between devices with their start and end apart: 1, of which 1 were waited for; matrix products, arithmetic and copies ran while one was open for 3% of the time, Pallas kernels for 0%

profile of v1, /device:TPU:0, one launch (start us, length us, event | category | flops | bytes accessed | tf_op | source)
XLA Modules:
  0.0 98.2 jit_solution(10640961663698709354)
XLA Ops:
  6.5 0.0 all-gather.3.cloned.1.call-start
  6.5 0.7 all-gather.3.cloned.1.call-update
  7.3 0.7 copy.18
  8.0 0.9 or_bitcast_fusion
  8.8 0.3 copy.10
  9.1 0.4 all_to_all.10
  9.5 12.0 %all_to_all.12 = s32[8,1,1536]{2,1,0:T(1,128)S(1)} all-to-all(s32[8,1,1536]{2,1,0:T(1,128)S(1)} %all_to_all.10), channel_id=1, replica_groups=mesh['grp'=4,'hh'=8] {'hh'}, dimensions={0} | all-to-all | bytes 98304 | tf_op jit(solution)/shard_map/all_to_all | solution.py:122
  21.5 0.6 copy.17
  22.1 37.4 %all-gather.3.cloned.1.call-done = bf16[2048,1024]{0,1:T(8,128)(2,1)} async-done(((bf16[256,1024]{0,1:T(8,128)(2,1)}), bf16[2048,1024]{0,1:T(8,128)(2,1)}) %all-gather.3.cloned.1.call-update) | async-done | bytes 4194320 | tf_op jit(solution)/shard_map/all_gather | solution.py:117
  59.5 6.4 %copy.12 = bf16[2048,1024]{1,0:T(8,128)(2,1)} copy(bf16[2048,1024]{0,1:T(8,128)(2,1)} %all-gather.3.cloned.1.call-done) | data formatting | bytes 8388608 | tf_op jit(solution)/shard_map/all_gather | solution.py:117
  65.9 25.5 %shard_map.55 = f32[192,256]{1,0:T(8,128)} custom-call(s32[8,1536]{1,0:T(8,128)} %bitcast.14, f32[192,256]{1,0:T(8,128)} %start_ref.1, bf16[8,256,1024]{2,1,0:T(8,128)(2,1)} %bitcast.12), custom_call_target="tpu_custom_call" | custom-call | tf_op jit(solution)/shard_map/pallas_call | solution.py:128
Async XLA Ops:
  6.5 52.9 %all-gather.3.cloned.1.call-start = ((), (), s32[]{:S(2)}) async-start(), calls=%async_computation.1 | async-start | bytes 4718592 | tf_op jit(solution)/shard_map/all_gather | solution.py:117
Sparse Core Ops, SparseCore 0:
  8.9 50.4 all-gather.2

commit v2 on v1

v2 whole, which is shorter than its diff:
```python
import functools

import jax
import jax.numpy as jnp
from jax import lax
from jax.experimental import pallas as pl
from jax.experimental.pallas import tpu as pltpu
from jax.sharding import PartitionSpec as P

conf_scale = 40.0
ridge_term = 16.0
small_eps = 1e-06
half_word = 16

NN = (((1,), (0,)), ((), ()))
NT = (((1,), (1,)), ((), ()))


def dot(left, right, dims=NN):
    return lax.dot_general(left, right, dims, preferred_element_type=jnp.float32)


def halves(value):
    high = value.astype(jnp.bfloat16)
    low = (value - high.astype(jnp.float32)).astype(jnp.bfloat16)
    return high, low


def stacked(value):
    return jnp.concatenate(halves(value), axis=0)


def folded(value):
    rows = value.shape[0] // 2
    return value[:rows] + value[rows:]


def gather(table, code, household_ids):
    trips = code >> half_word
    index = code & ((1 << half_word) - 1)
    weight = conf_scale * jnp.log1p(trips.astype(jnp.float32))
    live = (trips > 0).astype(jnp.float32)
    picked = None
    for quarter, piece in enumerate(table):
        ids = household_ids + quarter * household_ids.shape[0]
        onehot = (ids == index).astype(jnp.float32).astype(jnp.bfloat16)
        part = dot(piece, onehot)
        picked = part if picked is None else picked + part
    coef = (live * (1.0 + weight)).astype(jnp.bfloat16).astype(jnp.float32)
    return picked.astype(jnp.bfloat16), (weight * picked).astype(jnp.bfloat16), coef


def conjugate(start, gram_high, gram_low, rows_ref, weighted_ref, coef_ref, cap):
    groups, _, slots = rows_ref.shape
    per_group = start.shape[0] // groups
    lanes = per_group * cap
    row_ids = lax.broadcasted_iota(jnp.int32, (per_group, slots), 0)
    lane_ids = lax.broadcasted_iota(jnp.int32, (per_group, slots), 1)
    own = lax.rem(lane_ids, lanes) // cap == row_ids

    def spread(vector, from_coef):
        pieces = []
        for group in range(groups):
            part = vector[group * per_group : (group + 1) * per_group]
            inner = folded(dot(stacked(part), weighted_ref[group]))
            if from_coef:
                inner = coef_ref[group] - inner
            inner = jnp.where(own, inner, 0.0)
            pieces.append(folded(dot(stacked(inner), rows_ref[group], NT)))
        return jnp.concatenate(pieces, axis=0)

    def dense(vector):
        both = stacked(vector)
        return (
            folded(dot(both, gram_high))
            + dot(both[: vector.shape[0]], gram_low)
            + ridge_term * vector
        )

    answer = start
    resid = spread(answer, True) - dense(answer)
    direc = resid
    norm_now = jnp.sum(resid * resid, axis=-1, keepdims=True)
    for turn in range(2):
        image = dense(direc) + spread(direc, False)
        alpha = norm_now / (jnp.sum(direc * image, axis=-1, keepdims=True) + small_eps)
        answer = answer + alpha * direc
        if turn == 0:
            resid = resid - alpha * image
            norm_next = jnp.sum(resid * resid, axis=-1, keepdims=True)
            direc = resid + (norm_next / (norm_now + small_eps)) * direc
            norm_now = norm_next
    return answer


def solve_blocks(code_ref, start_ref, table_ref, out_ref, gram_high, gram_low, rows_ref, weighted_ref, coef_ref):
    sources, width, households = table_ref.shape
    groups = rows_ref.shape[0]
    lanes = code_ref.shape[1] // groups

    @pl.when(pl.program_id(0) == 0)
    def _():
        gram = dot(table_ref[0], table_ref[0], NT)
        for source in range(1, sources):
            gram = gram + dot(table_ref[source], table_ref[source], NT)
        gram_high[...], gram_low[...] = halves(gram)

    household_ids = lax.broadcasted_iota(jnp.int32, (households, lanes), 0)

    def fill(source):
        for group in range(groups):
            code = code_ref[pl.ds(source, 1), group * lanes : (group + 1) * lanes]
            place = pl.ds(pl.multiple_of(source * lanes, 128), lanes)
            rows, weighted, coef = gather([table_ref[source]], code, household_ids)
            rows_ref[group, :, place] = rows
            weighted_ref[group, :, place] = weighted
            coef_ref[group, :, place] = coef

    pl.loop(0, sources)(fill)
    cap = lanes * groups // start_ref.shape[0]
    out_ref[...] = conjugate(
        start_ref[...], gram_high[...], gram_low[...], rows_ref, weighted_ref, coef_ref, cap
    )


def exchange_and_solve(
    n_grp, n_hh, cores, code_ref, start_ref, shard_ref, out_ref, table, codes, gram_ref,
    rows_ref, weighted_ref, coef_ref, code_sems, shard_sems, line_sems, plane_sems, core_sems,
):
    grp, hh = lax.axis_index("grp"), lax.axis_index("hh")
    n_line = n_hh // cores
    line, core = hh // cores, lax.rem(hh, cores)
    twin = line * cores + lax.rem(core + 1, cores)
    _, quarters, width, piece_rows = table.shape
    groups = rows_ref.shape[0]
    lanes = code_ref.shape[2] // groups

    def remote(source, target, sems, place, device):
        return pltpu.make_async_remote_copy(
            src_ref=source,
            dst_ref=target,
            send_sem=sems.at[(0,) + place],
            recv_sem=sems.at[(1,) + place],
            device_id=device,
            device_id_type=pl.DeviceIdType.MESH,
        )

    barrier = pltpu.get_barrier_semaphore()
    for step in range(1, n_hh):
        pl.semaphore_signal(
            barrier, inc=1, device_id=(grp, lax.rem(hh + step, n_hh)), device_id_type=pl.DeviceIdType.MESH
        )
    for step in range(1, n_grp):
        pl.semaphore_signal(
            barrier, inc=1, device_id=(lax.rem(grp + step, n_grp), hh), device_id_type=pl.DeviceIdType.MESH
        )
    pl.semaphore_wait(barrier, n_hh + n_grp - 2)

    sent = []

    def send(copy):
        copy.start()
        sent.append(copy)

    def line_peer(step):
        return lax.rem(line + step, n_line) * cores + core

    def line_source(step, at_core):
        return lax.rem(line + n_line - step, n_line) * cores + at_core

    def plane_source(step):
        return lax.rem(grp + n_grp - step, n_grp)

    for step in range(1, n_line):
        send(remote(shard_ref.at[grp], table.at[hh, grp], line_sems, (step - 1,), (grp, line_peer(step))))
    send(remote(shard_ref, table.at[hh], shard_sems, (0,), (grp, twin)))
    for step in range(1, n_hh):
        target = lax.rem(hh + step, n_hh)
        send(remote(code_ref.at[target], codes.at[hh], code_sems, (step - 1,), (grp, target)))

    household_ids = lax.broadcasted_iota(jnp.int32, (piece_rows, lanes), 0)

    def fill(source, shard, code, first=False):
        gram = dot(shard[0], shard[0], NT)
        for quarter in range(1, quarters):
            gram = gram + dot(shard[quarter], shard[quarter], NT)
        if first:
            gram_ref[...] = gram
        else:
            gram_ref[...] += gram
        place = pl.ds(pl.multiple_of(source * lanes, 128), lanes)

        def fill_group(group):
            here = code[:, pl.ds(pl.multiple_of(group * lanes, 128), lanes)]
            rows, weighted, coef = gather([shard[q] for q in range(quarters)], here, household_ids)
            rows_ref[group, :, place] = rows
            weighted_ref[group, :, place] = weighted
            coef_ref[group, :, place] = coef

        pl.loop(0, groups)(fill_group)

    fill(hh, shard_ref, code_ref.at[hh], True)

    def forward_core(step, slot, quarter):
        piece = table.at[line_source(step, core), quarter]
        send(remote(piece, piece, core_sems, (step - 1, slot), (grp, twin)))

    for step in range(1, n_line):
        piece = table.at[line_source(step, core), grp]
        remote(piece, piece, line_sems, (step - 1,), (grp, hh)).wait_recv()
        for hop in range(1, n_grp):
            device = (lax.rem(grp + hop, n_grp), hh)
            send(remote(piece, piece, plane_sems, (step - 1, hop - 1), device))
        forward_core(step, 0, grp)

    for step in range(1, n_hh):
        target = lax.rem(hh + n_hh - step, n_hh)
        remote(codes.at[target], codes.at[target], code_sems, (step - 1,), (grp, hh)).wait_recv()

    remote(table.at[twin], table.at[twin], shard_sems, (0,), (grp, hh)).wait_recv()
    fill(twin, table.at[twin], codes.at[twin])

    def fill_twin(step):
        source = line_source(step, lax.rem(core + 1, cores))
        for slot in range(n_grp):
            piece = table.at[source, plane_source(slot)]
            remote(piece, piece, core_sems, (step - 1, slot), (grp, hh)).wait_recv()
        fill(source, table.at[source], codes.at[source])

    for step in range(1, n_line):
        source = line_source(step, core)
        for hop in range(1, n_grp):
            piece = table.at[source, plane_source(hop)]
            remote(piece, piece, plane_sems, (step - 1, hop - 1), (grp, hh)).wait_recv()
            forward_core(step, hop, plane_source(hop))
        if step > 1:
            fill_twin(step - 1)
        fill(source, table.at[source], codes.at[source])
    fill_twin(n_line - 1)

    gram_high, gram_low = halves(gram_ref[...])
    cap = lanes * groups // start_ref.shape[0]
    out_ref[...] = conjugate(
        start_ref[...], gram_high, gram_low, rows_ref, weighted_ref, coef_ref, cap
    )
    for copy in sent:
        copy.wait_send()


def shards(hh_factors, prod_init, hh_index, trips, counts):
    households, width = hh_factors.shape
    products = prod_init.shape[0]
    sources = lax.axis_size("hh")
    cap = hh_index.shape[4]
    slot_ids = lax.broadcasted_iota(jnp.int32, hh_index.shape, 4)
    live_trips = jnp.where(slot_ids < counts[..., None], trips, 0)
    code = (live_trips << half_word) | hh_index
    code = code.reshape(products, sources, cap).transpose(1, 0, 2).reshape(sources, products * cap)
    cores = 2
    n_grp = lax.axis_size("grp")
    per_group = 64 if products % 64 == 0 else products
    lanes = per_group * cap
    fits = products * sources * cap <= 16384 and sources % cores == 0
    block = products if fits else per_group
    groups = block // per_group
    wide = (groups, width, sources * lanes)
    gathered = [
        pltpu.VMEM(wide, jnp.bfloat16),
        pltpu.VMEM(wide, jnp.bfloat16),
        pltpu.VMEM((groups, 1, sources * lanes), jnp.float32),
    ]
    answer_shape = jax.ShapeDtypeStruct(prod_init.shape, jnp.float32)
    if fits:
        piece_rows = households // n_grp
        shard = hh_factors.reshape(n_grp, piece_rows, width).transpose(0, 2, 1)
        n_line = sources // cores
        dma = pltpu.SemaphoreType.DMA
        return pl.pallas_call(
            functools.partial(exchange_and_solve, n_grp, sources, cores),
            out_shape=answer_shape,
            in_specs=[pl.BlockSpec(memory_space=pltpu.VMEM)] * 3,
            out_specs=pl.BlockSpec(memory_space=pltpu.VMEM),
            scratch_shapes=[
                pltpu.VMEM((sources, n_grp, width, piece_rows), jnp.bfloat16),
                pltpu.VMEM((sources, 1, products * cap), jnp.int32),
                pltpu.VMEM((width, width), jnp.float32),
                *gathered,
                dma((2, sources - 1)),
                dma((2, 1)),
                dma((2, n_line - 1)),
                dma((2, n_line - 1, n_grp - 1)),
                dma((2, n_line - 1, n_grp)),
            ],
            compiler_params=pltpu.CompilerParams(
                collective_id=0, has_side_effects=True, vmem_limit_bytes=60 * 2**20
            ),
        )(code.reshape(sources, 1, products * cap), prod_init, shard)

    table = lax.all_gather(hh_factors.T, "hh", axis=0)
    code = lax.all_to_all(code, "hh", split_axis=0, concat_axis=0, tiled=True)
    return pl.pallas_call(
        solve_blocks,
        grid=(products // block,),
        out_shape=answer_shape,
        in_specs=[
            pl.BlockSpec((sources, block * cap), lambda i: (0, i)),
            pl.BlockSpec((block, width), lambda i: (i, 0)),
            pl.BlockSpec(memory_space=pltpu.VMEM),
        ],
        out_specs=pl.BlockSpec((block, width), lambda i: (i, 0)),
        scratch_shapes=[
            pltpu.VMEM((width, width), jnp.bfloat16),
            pltpu.VMEM((width, width), jnp.bfloat16),
            *gathered,
        ],
        compiler_params=pltpu.CompilerParams(vmem_limit_bytes=60 * 2**20),
    )(code, prod_init, table)


def solution(mesh):
    placed = (
        P("hh", None),
        P(("grp", "hh"), None),
        P("grp", None, None, "hh", None),
        P("grp", None, None, "hh", None),
        P("grp", None, None, "hh"),
    )
    return jax.shard_map(
        shards, mesh=mesh, in_specs=placed, out_specs=P(("grp", "hh"), None), check_vma=False
    )
```

time: 98.6 us -> 54.8 us (0.56)
  waiting for transfers between devices: 38.1 us -> 0 us
  Pallas kernels: 25.5 us -> 48.3 us
  between operations: 13.4 us -> 0.03 us
  blocking collectives: 12 us -> 0 us
  local copies, waits for them, and re-layouts: 8.43 us -> 4.61 us
    all_gather x1 -> x0, waiting for transfers between devices: 37.4 us -> none  [shards(): table = lax.all_gather(hh_factors.T, 'hh', axis=0)]
    pallas_call x1, Pallas kernels: 25.5 us -> 48.3 us  [shards(): pl.pallas_call(functools.partial(exchange_and_solve, n_grp, sources, core...]
    all_to_all x1 -> x0, blocking collectives: 12 us -> none  [shards(): code = lax.all_to_all(code, 'hh', split_axis=0, concat_axis=0, tiled=True)]
    all_gather x1 -> x0, local copies, waits for them, and re-layouts: 6.42 us -> none  [shards(): table = lax.all_gather(hh_factors.T, 'hh', axis=0)]
    another operation x0 -> x1, local copies, waits for them, and re-layouts: none -> 1.02 us  [shards(): code.reshape(sources, 1, products * cap)]
    unnamed x2 -> x4, local copies, waits for them, and re-layouts: 1.33 us -> 2.33 us
    reshape x0 -> x1, local copies, waits for them, and re-layouts: none -> 0.99 us  [shards(): shard = hh_factors.reshape(n_grp, piece_rows, width).transpose(0, 2, 1)]
  transfers between devices with their start and end apart: 1 -> 0, of which waited for: 1 -> 0; matrix products, arithmetic and copies ran while one was open for 3% -> 0% of each run, Pallas kernels for 0% -> 0%
where the time goes in v2:
time: 54.8 us; the launch traced here: 53.9 us
  Pallas kernels  48.3 us (88%)
  local copies, waits for them, and re-layouts  4.61 us (8%)
  other arithmetic  0.89 us (2%)
    pallas_call x1, Pallas kernels, shards(): pl.pallas_call(functools.partial(exchange_and_solve, n_grp, sources, core...  48.3 us
    unnamed x4, local copies, waits for them, and re-layouts  2.33 us

profile of v2, /device:TPU:0, one launch (start us, length us, event | category | flops | bytes accessed | tf_op | source)
XLA Modules:
  0.0 53.9 jit_solution(11748048580431478185)
XLA Ops:
  0.0 0.7 %copy.12 = s32[1,192,8,1]{1,2,3,0:T(8,128)S(1)} copy(s32[1,192,8,1]{1,3,2,0:T(1,128)} %param.9) | data formatting | bytes 12288
  0.7 0.9 %or_bitcast_fusion = s32[8,192,8]{1,2,0:T(8,128)S(1)} fusion(s32[1,192,8,1,8]{1,4,3,2,0:T(8,128)} %param.7, s32[1,192,8,1,8]{1,4,3,2,0:T(8,128)} %param.8, s32[192,8]{0,1:T(8,128)S(1)} %bitcast.11), kind=kLoop, calls=%fused_computation | loop fusion | flops 49152 | bytes 153600 | tf_op jit(solution)/shard_map/transpose | solution.py:258
  1.6 0.3 copy.7
  1.9 0.0 copy-start
  1.9 1.0 %reshape_reshape.4.code_ref = s32[8,1,1536]{2,1,0:T(1,128)} reshape(s32[8,192,8]{2,1,0:T(8,128)S(1)} %copy.7) | data formatting | bytes 98304 | tf_op jit(solution)/shard_map/reshape;reshape | solution.py:297
  2.9 0.0 copy-done
  2.9 1.0 %copy.8 = bf16[4,256,256]{1,2,0:T(8,128)(2,1)} copy(bf16[4,256,256]{2,1,0:T(8,128)(2,1)S(1)} %bitcast.10) | data formatting | bytes 1048576 | tf_op jit(solution)/shard_map/reshape | solution.py:275
  3.9 48.3 %shard_map.55 = f32[192,256]{1,0:T(8,128)} custom-call(s32[8,1,1536]{2,1,0:T(1,128)} %reshape_reshape.4.code_ref, f32[192,256]{1,0:T(8,128)} %start_ref.1, bf16[4,256,256]{2,1,0:T(8,128)(2,1)} %bitcast.9), custom_call_target="tpu_custom_call" | custom-call | tf_op jit(solution)/shard_map/pallas_call | solution.py:278
  52.2 1.6 %copy.14 = f32[192,256]{1,0:T(8,128)} copy(f32[192,256]{1,0:T(8,128)} %shard_map.55) | data formatting | bytes 393216
Async XLA Ops:
  1.9 1.0 %copy-start = (bf16[1024,256]{1,0:T(8,128)(2,1)S(1)}, bf16[1024,256]{1,0:T(8,128)(2,1)}, u32[]{:S(2)}) copy-start(bf16[1024,256]{1,0:T(8,128)(2,1)} %param.5) | copy-start | bytes 1572868

commit v3 on v2

--- a/solution.py
+++ b/solution.py
@@ -47,16 +47,18 @@
         part = dot(piece, onehot)
         picked = part if picked is None else picked + part
     coef = (live * (1.0 + weight)).astype(jnp.bfloat16).astype(jnp.float32)
-    return picked.astype(jnp.bfloat16), (weight * picked).astype(jnp.bfloat16), coef
+    return picked.T.astype(jnp.bfloat16), (weight * picked).astype(jnp.bfloat16), coef
 
 
 def conjugate(start, gram_high, gram_low, rows_ref, weighted_ref, coef_ref, cap):
-    groups, _, slots = rows_ref.shape
+    groups, slots, _ = rows_ref.shape
     per_group = start.shape[0] // groups
     lanes = per_group * cap
-    row_ids = lax.broadcasted_iota(jnp.int32, (per_group, slots), 0)
-    lane_ids = lax.broadcasted_iota(jnp.int32, (per_group, slots), 1)
-    own = lax.rem(lane_ids, lanes) // cap == row_ids
+    row_ids = lax.broadcasted_iota(jnp.int32, (per_group, lanes), 0)
+    lane_ids = lax.broadcasted_iota(jnp.int32, (per_group, lanes), 1)
+    first = row_ids * cap
+    inside = jnp.logical_and(lane_ids >= first, lane_ids < first + cap)
+    own = jnp.concatenate([inside.astype(jnp.float32)] * (slots // lanes), axis=1) > 0.0
 
     def spread(vector, from_coef):
         pieces = []
@@ -66,7 +68,7 @@
             if from_coef:
                 inner = coef_ref[group] - inner
             inner = jnp.where(own, inner, 0.0)
-            pieces.append(folded(dot(stacked(inner), rows_ref[group], NT)))
+            pieces.append(folded(dot(stacked(inner), rows_ref[group])))
         return jnp.concatenate(pieces, axis=0)
 
     def dense(vector):
@@ -112,7 +114,7 @@
             code = code_ref[pl.ds(source, 1), group * lanes : (group + 1) * lanes]
             place = pl.ds(pl.multiple_of(source * lanes, 128), lanes)
             rows, weighted, coef = gather([table_ref[source]], code, household_ids)
-            rows_ref[group, :, place] = rows
+            rows_ref[group, place, :] = rows
             weighted_ref[group, :, place] = weighted
             coef_ref[group, :, place] = coef
 
@@ -193,7 +195,7 @@
         def fill_group(group):
             here = code[:, pl.ds(pl.multiple_of(group * lanes, 128), lanes)]
             rows, weighted, coef = gather([shard[q] for q in range(quarters)], here, household_ids)
-            rows_ref[group, :, place] = rows
+            rows_ref[group, place, :] = rows
             weighted_ref[group, :, place] = weighted
             coef_ref[group, :, place] = coef
 
@@ -265,7 +267,7 @@
     groups = block // per_group
     wide = (groups, width, sources * lanes)
     gathered = [
-        pltpu.VMEM(wide, jnp.bfloat16),
+        pltpu.VMEM((groups, sources * lanes, width), jnp.bfloat16),
         pltpu.VMEM(wide, jnp.bfloat16),
         pltpu.VMEM((groups, 1, sources * lanes), jnp.float32),
     ]

time: 54.8 us -> 49.9 us (0.911)
  the two profiles are of different devices: /device:TPU:0 before, /device:TPU:24 now
where the time goes in v3:
time: 49.9 us; the launch traced here: 49.6 us
  Pallas kernels  44.1 us (88%)
  local copies, waits for them, and re-layouts  4.61 us (9%)
  other arithmetic  0.89 us (2%)
    pallas_call x1, Pallas kernels, shards(): pl.pallas_call(functools.partial(exchange_and_solve, n_grp, sources, core...  44.1 us
    unnamed x4, local copies, waits for them, and re-layouts  2.33 us
    another operation x1, local copies, waits for them, and re-layouts, shards(): code.reshape(sources, 1, products * cap)  1.02 us

profile of v3, /device:TPU:24, one launch (start us, length us, event | category | flops | bytes accessed | tf_op | source)
XLA Modules:
  0.0 49.6 jit_solution(6749858025022575261)
XLA Ops:
  0.0 0.7 %copy.12 = s32[1,192,8,1]{1,2,3,0:T(8,128)S(1)} copy(s32[1,192,8,1]{1,3,2,0:T(1,128)} %param.9) | data formatting | bytes 12288
  0.7 0.9 %or_bitcast_fusion = s32[8,192,8]{1,2,0:T(8,128)S(1)} fusion(s32[1,192,8,1,8]{1,4,3,2,0:T(8,128)} %param.7, s32[1,192,8,1,8]{1,4,3,2,0:T(8,128)} %param.8, s32[192,8]{0,1:T(8,128)S(1)} %bitcast.11), kind=kLoop, calls=%fused_computation | loop fusion | flops 49152 | bytes 153600 | tf_op jit(solution)/shard_map/transpose | solution.py:260
  1.6 0.3 copy.7
  1.9 0.0 copy-start
  1.9 1.0 %reshape_reshape.4.code_ref = s32[8,1,1536]{2,1,0:T(1,128)} reshape(s32[8,192,8]{2,1,0:T(8,128)S(1)} %copy.7) | data formatting | bytes 98304 | tf_op jit(solution)/shard_map/reshape;reshape | solution.py:299
  2.9 0.0 copy-done
  2.9 1.0 %copy.8 = bf16[4,256,256]{1,2,0:T(8,128)(2,1)} copy(bf16[4,256,256]{2,1,0:T(8,128)(2,1)S(1)} %bitcast.10) | data formatting | bytes 1048576 | tf_op jit(solution)/shard_map/reshape | solution.py:277
  3.9 44.1 %shard_map.55 = f32[192,256]{1,0:T(8,128)} custom-call(s32[8,1,1536]{2,1,0:T(1,128)} %reshape_reshape.4.code_ref, f32[192,256]{1,0:T(8,128)} %start_ref.1, bf16[4,256,256]{2,1,0:T(8,128)(2,1)} %bitcast.9), custom_call_target="tpu_custom_call" | custom-call | tf_op jit(solution)/shard_map/pallas_call | solution.py:280
  48.0 1.6 %copy.14 = f32[192,256]{1,0:T(8,128)} copy(f32[192,256]{1,0:T(8,128)} %shard_map.55) | data formatting | bytes 393216
Async XLA Ops:
  1.9 1.0 %copy-start = (bf16[1024,256]{1,0:T(8,128)(2,1)S(1)}, bf16[1024,256]{1,0:T(8,128)(2,1)}, u32[]{:S(2)}) copy-start(bf16[1024,256]{1,0:T(8,128)(2,1)} %param.5) | copy-start | bytes 1572868
